TPU v7x, 128 devices: a whole 4x4x4 slice. The times are simulated.
128 devices in a mesh: row: 16 (over y_lo, z, core), col: 8 (over y_hi, x).
Axes of the slice: x: 4, y: 4 (y_hi: 2, y_lo: 2; y = y_hi * 2 + y_lo), z: 4, core: 2. Of those that a mesh axis runs over, the one named last changes fastest.
Arguments:
- features: bfloat16 [65536, 512], P(('row', 'col')), may hold values from -6 to 6
- partition_of: int32 [65536], P(('row', 'col')), may hold values from 0 to 127, as said below
- weight: bfloat16 [512, 512], replicated, may hold values from -0.25 to 0.25
- tile_values: bfloat16 [16, 8, 192, 128, 128], P('row', 'col'), may hold values from -0.109375 to 0.109375
- tile_rows: int32 [16, 8, 192], P('row', 'col'), may hold values from 0 to 31
- tile_cols: int32 [16, 8, 192], P('row', 'col'), may hold values from 0 to 63
- tile_count: int32 [16, 8], P('row', 'col'), may hold values from 48 to 192, as said below
- out_cotangent: bfloat16 [65536, 512], P('row'), may hold values from -6 to 6
Outputs:
- activations: bfloat16 [65536, 512], P(('row', 'col'))
- weight_grad: float32 [512, 512], replicated
Inputs may be any that keep to these rules, and one draw needn't show every extreme that they name: `partition_of`: of the 512 regions of each device in detection order, exactly 4 go to each partition. `tile_count`: some grid position has all 192 slots live in every draw.
All inputs are finite; a program needn't handle non-finite values.
Results may differ from a plain program's by a relative error of at most 0.005.
Values may be sent and summed in bfloat16 or wider, within the bound.
No kernel may reach another device: no remote copies, remote signals or barrier semaphores. Data moves between devices by JAX's collectives and lax.ppermute only.
A program may use at most 192 MiB of HBM per device.

v0:
```python
import math
import jax
import jax.numpy as jnp
from jax import lax
from jax.sharding import PartitionSpec as P


def silu_slope(pre):
    sigmoid = jax.nn.sigmoid(pre)
    return sigmoid * (1.0 + pre * (1.0 - sigmoid))


def regroup(features, partition_of, n_row, n_col):
    slots, feature_width = features.shape
    per_peer = slots // (n_row * n_col)
    ordering = jnp.argsort(partition_of, stable=True)
    outgoing = features[ordering]
    shaped = outgoing.reshape(n_row * n_col, per_peer, feature_width)
    arrived = lax.all_to_all(shaped, ("row", "col"), split_axis=0, concat_axis=0, tiled=True)
    return arrived.reshape(slots, feature_width)


def tile_products(blocks, row_index, column_index, live_count, sources, out_tiles, forward):
    tile_size = blocks.shape[-1]
    feature_width = sources.shape[-1]
    source_tiles = sources.reshape(-1, tile_size, feature_width)
    empty = jnp.zeros((out_tiles, tile_size, feature_width), jnp.float32)
    block_total = (live_count + 31) // 32

    def one_block(block_step, totals):
        first_slot = block_step * 32
        tile_block = lax.dynamic_slice_in_dim(blocks, first_slot, 32, 0)
        row_part = lax.dynamic_slice_in_dim(row_index, first_slot, 32, 0)
        column_part = lax.dynamic_slice_in_dim(column_index, first_slot, 32, 0)
        is_live = first_slot + jnp.arange(32, dtype=jnp.int32) < live_count
        tile_block = jnp.where(is_live[:, None, None], tile_block, jnp.zeros_like(tile_block))
        if forward:
            picked = source_tiles[column_part]
            products = jnp.einsum(
                "tij,tjf->tif", tile_block, picked, preferred_element_type=jnp.float32
            )
            return totals.at[row_part].add(products)
        picked = source_tiles[row_part]
        products = jnp.einsum(
            "tij,tif->tjf", tile_block, picked, preferred_element_type=jnp.float32
        )
        return totals.at[column_part].add(products)

    totals = lax.fori_loop(0, block_total, one_block, empty)
    return totals.reshape(out_tiles * tile_size, feature_width)


def shards(
    features, partition_of, weight, tile_values, tile_rows, tile_cols, tile_count, out_cotangent
):
    n_row = lax.axis_size("row")
    n_col = lax.axis_size("col")
    regrouped = regroup(features, partition_of, n_row, n_col)
    slots, feature_width = regrouped.shape
    tile_size = tile_values.shape[-1]
    blocks = tile_values.reshape(-1, tile_size, tile_size)
    row_index = tile_rows.reshape(-1)
    column_index = tile_cols.reshape(-1)
    live_count = tile_count.reshape(())
    row_tiles = slots * n_col // tile_size
    column_tiles = slots * n_row // tile_size
    hidden = jnp.dot(regrouped, weight, preferred_element_type=jnp.float32).astype(jnp.bfloat16)
    hidden_columns = lax.all_gather(hidden, "row", axis=0, tiled=True)
    partial_value = tile_products(
        blocks, row_index, column_index, live_count, hidden_columns, row_tiles, True
    )
    position = lax.axis_index("col") * slots
    pre = lax.psum(partial_value, "col")
    own_pre = lax.dynamic_slice_in_dim(pre, position, slots, 0)
    activations = jax.nn.silu(own_pre).astype(jnp.bfloat16)
    slope = (out_cotangent.astype(jnp.float32) * silu_slope(pre)).astype(jnp.bfloat16)
    back_partial = tile_products(
        blocks, row_index, column_index, live_count, slope, column_tiles, False
    )
    hidden_grad = lax.psum_scatter(back_partial, "row", scatter_dimension=0, tiled=True)
    local_grad = jnp.dot(
        regrouped.astype(jnp.float32).T,
        hidden_grad,
        precision=lax.Precision.HIGHEST,
        preferred_element_type=jnp.float32,
    )
    weight_grad = lax.psum(local_grad, ("row", "col")) * (1.0 / math.sqrt(slots * n_row * n_col))
    return (activations, weight_grad)


def solution(mesh):
    placed = (
        P(("row", "col"), None),
        P(("row", "col")),
        P(),
        P("row", "col", None, None, None),
        P("row", "col", None),
        P("row", "col", None),
        P("row", "col"),
        P("row", None),
    )
    return jax.shard_map(
        shards,
        mesh=mesh,
        in_specs=placed,
        out_specs=(P(("row", "col"), None), P()),
        check_vma=False,
    )
```

profile of v0, /device:TPU:1, one launch (start us, length us, event | category | flops | bytes accessed | tf_op | source)
XLA Modules:
  0.0 937.0 jit_solution(18352285362092890931)
XLA Ops:
  13.9 23.8 %all_to_all.5 = bf16[128,4,512]{2,1,0:T(4,128)(2,1)S(1)} all-to-all(bf16[128,4,512]{2,1,0:T(4,128)(2,1)S(1)} %reshape.48), channel_id=1, replica_groups=mesh['row'=16,'col'=8] {'row','col'}, dimensions={0} | all-to-all | bytes 1048576 | tf_op jit(solution)/shard_map/all_to_all | solution.py:19
  41.1 49.4 %all-gather.2.cloned.1.call-done = bf16[8192,512]{1,0:T(8,128)(2,1)} async-done(((bf16[512,512]{1,0:T(8,128)(2,1)}), bf16[8192,512]{1,0:T(8,128)(2,1)}) %all-gather.2.cloned.1.call-update) | async-done | bytes 8388624 | tf_op jit(solution)/shard_map/all_gather | solution.py:68
  94.8 97.0 %while.20 = (s32[]{:T(128)}, f32[32,128,512]{2,1,0:T(8,128)}, s32[]{:T(128)}, s32[192]{0:T(256)S(1)}, s32[]{:T(128)}, /*index=5*/bf16[192,128,128]{2,1,0:T(8,128...) while((s32[]{:T(128)}, f32[32,128,512]{2,1,0:T(8,128)}, ...), condition=%wide.region_3.4_spmd, body=%wide.region_1.3_spmd.sunk | while | flops 539493632 | bytes 47191152 | solution.py:49
  95.6 6.1 gather_fusion
  101.7 7.0 fusion.29
  108.7 18.8 %scatter_fusion = f32[32,128,512]{2,1,0:T(8,128)} fusion(f32[32,128,512]{2,1,0:T(8,128)} %get-tuple-element.257, s32[32]{0:T(128)S(1)} %get-tuple-element.232, f32[32,128,512]{2,1,0:T(8,128)} %fusion.29), kind=kCustom, calls=%fused_computation.3.clone.1 | custom fusion | flops 2097152 | bytes 25165952 | tf_op jit(solution)/shard_map/while/body/scatter-add | solution.py:42
  128.3 6.1 gather_fusion
  134.4 7.0 fusion.29
  141.4 18.5 %scatter_fusion = f32[32,128,512]{2,1,0:T(8,128)} fusion(f32[32,128,512]{2,1,0:T(8,128)} %get-tuple-element.257, s32[32]{0:T(128)S(1)} %get-tuple-element.232, f32[32,128,512]{2,1,0:T(8,128)} %fusion.29), kind=kCustom, calls=%fused_computation.3.clone.1 | custom fusion | flops 2097152 | bytes 25165952 | tf_op jit(solution)/shard_map/while/body/scatter-add | solution.py:42
  166.7 7.0 fusion.29
  173.7 18.1 %scatter_fusion = f32[32,128,512]{2,1,0:T(8,128)} fusion(f32[32,128,512]{2,1,0:T(8,128)} %get-tuple-element.257, s32[32]{0:T(128)S(1)} %get-tuple-element.232, f32[32,128,512]{2,1,0:T(8,128)} %fusion.29), kind=kCustom, calls=%fused_computation.3.clone.1 | custom fusion | flops 2097152 | bytes 25165952 | tf_op jit(solution)/shard_map/while/body/scatter-add | solution.py:42
  191.9 8.6 copy.10
  200.5 275.5 %all-reduce.3.cloned.1.call-done = f32[4096,512]{1,0:T(8,128)} async-done(((f32[4096,512]{1,0:T(8,128)}), f32[4096,512]{1,0:T(8,128)}) %all-reduce.3.cloned.1.call-update) | async-done | bytes 8388624 | tf_op jit(solution)/shard_map/psum | solution.py:73
  476.0 7.6 multiply_convert_fusion
  483.7 7.9 broadcast_in_dim.38
  491.5 94.5 %while.21 = (s32[]{:T(128)}, f32[64,128,512]{2,1,0:T(8,128)}, s32[]{:T(128)}, s32[192]{0:T(256)S(1)}, s32[]{:T(128)}, /*index=5*/bf16[192,128,128]{1,2,0:T(8,128...) while((s32[]{:T(128)}, f32[64,128,512]{2,1,0:T(8,128)}, ...), condition=%wide.region_7.8_spmd, body=%wide.region_5.7_spmd.sunk | while | flops 539493632 | bytes 47191152 | solution.py:49
  497.4 7.0 fusion.32
  504.4 18.6 %scatter_fusion.1 = f32[64,128,512]{2,1,0:T(8,128)} fusion(f32[64,128,512]{2,1,0:T(8,128)} %get-tuple-element.293, s32[32]{0:T(128)S(1)} %get-tuple-element.242, f32[32,128,512]{2,1,0:T(8,128)} %fusion.32), kind=kCustom, calls=%fused_computation.4.clone.1 | custom fusion | flops 2097152 | bytes 25165952 | tf_op jit(solution)/shard_map/while/body/scatter-add | solution.py:47
  528.8 7.0 fusion.32
  535.8 18.6 %scatter_fusion.1 = f32[64,128,512]{2,1,0:T(8,128)} fusion(f32[64,128,512]{2,1,0:T(8,128)} %get-tuple-element.293, s32[32]{0:T(128)S(1)} %get-tuple-element.242, f32[32,128,512]{2,1,0:T(8,128)} %fusion.32), kind=kCustom, calls=%fused_computation.4.clone.1 | custom fusion | flops 2097152 | bytes 25165952 | tf_op jit(solution)/shard_map/while/body/scatter-add | solution.py:47
  560.3 7.0 fusion.32
  567.3 18.7 %scatter_fusion.1 = f32[64,128,512]{2,1,0:T(8,128)} fusion(f32[64,128,512]{2,1,0:T(8,128)} %get-tuple-element.293, s32[32]{0:T(128)S(1)} %get-tuple-element.242, f32[32,128,512]{2,1,0:T(8,128)} %fusion.32), kind=kCustom, calls=%fused_computation.4.clone.1 | custom fusion | flops 2097152 | bytes 25165952 | tf_op jit(solution)/shard_map/while/body/scatter-add | solution.py:47
  586.1 189.1 %reduce-scatter.2.cloned.1.call-done = f32[512,512]{1,0:T(8,128)} async-done(((f32[8192,512]{1,0:T(8,128)}), f32[512,512]{1,0:T(8,128)}) %reduce-scatter.2.cloned.1.call-update) | async-done | bytes 1048592 | tf_op jit(solution)/shard_map/reduce_scatter | solution.py:80
  780.8 147.3 %all-reduce.5.cloned.1.call-done = f32[512,512]{1,0:T(8,128)} async-done(((f32[512,512]{1,0:T(8,128)}), f32[512,512]{1,0:T(8,128)}) %all-reduce.5.cloned.1.call-update) | async-done | bytes 1048592 | tf_op jit(solution)/shard_map/psum | solution.py:87
  (54 shorter events, 47.4 us)
Async XLA Ops:
  7.2 4.6 copy-start
  7.2 83.3 %all-gather.2.cloned.1.call-start = ((), (), s32[]{:S(2)}) async-start(), calls=%async_computation.2 | async-start | bytes 8912896 | tf_op jit(solution)/shard_map/all_gather | solution.py:68
  11.7 83.0 %copy-start.4 = (s32[1,1,192]{2,1,0:T(1,128)S(1)}, s32[1,1,192]{2,1,0:T(1,128)}, u32[]{:S(2)}) copy-start(s32[1,1,192]{2,1,0:T(1,128)} %param.16) | copy-start | bytes 2308
  11.8 83.0 %copy-start.5 = (s32[1,1,192]{2,1,0:T(1,128)S(1)}, s32[1,1,192]{2,1,0:T(1,128)}, u32[]{:S(2)}) copy-start(s32[1,1,192]{2,1,0:T(1,128)} %param.17) | copy-start | bytes 2308
  37.9 56.9 %copy-start.2 = (bf16[512,512]{1,0:T(8,128)(2,1)}, bf16[512,512]{1,0:T(8,128)(2,1)S(1)}, u32[]{:S(2)}) copy-start(bf16[512,512]{1,0:T(8,128)(2,1)S(1)} %reshape.49) | copy-start | bytes 1572868
  40.4 435.7 %all-reduce.3.cloned.1.call-start = ((), (), s32[]{:S(2)}) async-start(), calls=%async_computation.3 | async-start | bytes 16777216 | tf_op jit(solution)/shard_map/psum | solution.py:73
  191.8 583.4 %reduce-scatter.2.cloned.1.call-start = ((), (), s32[]{:S(2)}) async-start(), calls=%async_computation.4 | async-start | bytes 17825792 | tf_op jit(solution)/shard_map/reduce_scatter | solution.py:80
  586.0 344.4 %copy-start.1 = (bf16[512,512]{1,0:T(8,128)(2,1)S(1)}, bf16[512,512]{1,0:T(8,128)(2,1)}, u32[]{:S(2)}) copy-start(bf16[512,512]{1,0:T(8,128)(2,1)} %param.12) | copy-start | bytes 1572868
  586.0 189.2 %copy-start.3 = (bf16[512,512]{1,0:T(8,128)(2,1)S(1)}, bf16[512,512]{1,0:T(8,128)(2,1)}, u32[]{:S(2)}) copy-start(bf16[512,512]{1,0:T(8,128)(2,1)} %copy-done.2) | copy-start | bytes 1572868
  586.1 342.1 %all-reduce.5.cloned.1.call-start = ((), (), s32[]{:S(2)}) async-start(), calls=%async_computation.5 | async-start | bytes 2097152 | tf_op jit(solution)/shard_map/psum | solution.py:87
Sparse Core Ops, SparseCore 0:
  40.5 49.9 all-gather.1
  192.0 284.0 all-reduce.2
  586.2 188.9 reduce-scatter.1
  780.4 147.6 all-reduce.4
where the time goes:
time: 939 us; the launch traced here: 937 us
  waiting for transfers between devices  661 us (70%)
  other arithmetic  132 us (14%)
  local copies, waits for them, and re-layouts  56.7 us (6%)
  matrix products  47.8 us (5%)
  blocking collectives  23.8 us (3%)
  between operations  14.5 us (2%)
    psum x1, waiting for transfers between devices, shards(): pre = lax.psum(partial_value, 'col')  276 us
    reduce_scatter x1, waiting for transfers between devices, shards(): lax.psum_scatter(back_partial, 'row', scatter_dimension=0, tiled=True)  189 us
    psum x1, waiting for transfers between devices, shards(): lax.psum(local_grad, ('row', 'col'))  147 us
    scatter-add x3, other arithmetic, one_block(): return totals.at[column_part].add(products)  55.9 us
    scatter-add x3, other arithmetic, one_block(): return totals.at[row_part].add(products)  55.4 us
    all_gather x1, waiting for transfers between devices, shards(): hidden_columns = lax.all_gather(hidden, 'row', axis=0, tiled=True)  49.4 us
    all_to_all x1, blocking collectives, regroup(): lax.all_to_all(shaped, ('row', 'col'), split_axis=0, concat_axis=0, tiled...  23.8 us
    dot_general x3, matrix products, one_block(): jnp.einsum('tij,tjf->tif', tile_block, picked, preferred_element_type=jnp...  21.1 us
  transfers between devices with their start and end apart: 4, of which 4 were waited for; matrix products, arithmetic and copies ran while one was open for 1% of the time, Pallas kernels for 0%

commit v1 on v0

--- a/solution.py
+++ b/solution.py
@@ -65,7 +65,9 @@
     row_tiles = slots * n_col // tile_size
     column_tiles = slots * n_row // tile_size
     hidden = jnp.dot(regrouped, weight, preferred_element_type=jnp.float32).astype(jnp.bfloat16)
-    hidden_columns = lax.all_gather(hidden, "row", axis=0, tiled=True)
+    hidden_columns = jnp.concatenate(
+        lax.all_to_all(jnp.stack([hidden] * lax.axis_size("row")), "row", 0, 0), axis=0
+    )
     partial_value = tile_products(
         blocks, row_index, column_index, live_count, hidden_columns, row_tiles, True
     )

time: 939 us -> 1020 us (1.086)
  waiting for transfers between devices: 661 us -> 736 us
    all_to_all x0 -> x1, waiting for transfers between devices: none -> 120 us  [shards(): lax.all_to_all(jnp.stack([hidden] * lax.axis_size('row')), 'row', 0, 0)]
    all_gather x1 -> x0, waiting for transfers between devices: 49.4 us -> none  [shards(): hidden_columns = lax.all_gather(hidden, 'row', axis=0, tiled=True)]
where the time goes in v1:
time: 1020 us
  waiting for transfers between devices  736 us (72%)
  other arithmetic  132 us (13%)
  local copies, waits for them, and re-layouts  60.7 us (6%)
  matrix products  47 us (5%)
  blocking collectives  23.8 us (2%)
  between operations  14.5 us (1%)
    psum x1, waiting for transfers between devices, shards(): pre = lax.psum(partial_value, 'col')  279 us
    reduce_scatter x1, waiting for transfers between devices, shards(): lax.psum_scatter(back_partial, 'row', scatter_dimension=0, tiled=True)  189 us
    psum x1, waiting for transfers between devices, shards(): lax.psum(local_grad, ('row', 'col'))  147 us
    all_to_all x1, waiting for transfers between devices, shards(): lax.all_to_all(jnp.stack([hidden] * lax.axis_size('row')), 'row', 0, 0)  120 us
    scatter-add x3, other arithmetic, one_block(): return totals.at[column_part].add(products)  55.9 us
    scatter-add x3, other arithmetic, one_block(): return totals.at[row_part].add(products)  55.4 us
    all_to_all x1, blocking collectives, regroup(): lax.all_to_all(shaped, ('row', 'col'), split_axis=0, concat_axis=0, tiled...  23.8 us
    dot_general x3, matrix products, one_block(): jnp.einsum('tij,tjf->tif', tile_block, picked, preferred_element_type=jnp...  21 us
  transfers between devices with their start and end apart: 4, of which 4 were waited for; matrix products, arithmetic and copies ran while one was open for 1% of the time, Pallas kernels for 0%

profile of v1, /device:TPU:1, one launch (start us, length us, event | category | flops | bytes accessed | tf_op | source)
XLA Modules:
  0.0 1020.7 jit_solution(18345518472371773010)
XLA Ops:
  13.8 23.8 %all_to_all.10 = bf16[128,4,512]{2,1,0:T(4,128)(2,1)S(1)} all-to-all(bf16[128,4,512]{2,1,0:T(4,128)(2,1)S(1)} %reshape.47), channel_id=1, replica_groups=mesh['row'=16,'col'=8] {'row','col'}, dimensions={0} | all-to-all | bytes 1048576 | tf_op jit(solution)/shard_map/all_to_all | solution.py:19
  50.3 120.1 %all-to-all-done.1 = bf16[16,512,512]{2,1,0:T(8,128)(2,1)} async-done(((bf16[16,512,512]{2,1,0:T(8,128)(2,1)}), bf16[16,512,512]{2,1,0:T(8,128)(2,1)}, u32[]{:S(2)}, u32[]{:S(2)}) %all-to-all-start.1) | async-done | bytes 8388640 | tf_op jit(solution)/shard_map/all_to_all | solution.py:69
  174.8 97.0 %while.20 = (s32[]{:T(128)}, f32[32,128,512]{2,1,0:T(8,128)}, s32[]{:T(128)}, s32[192]{0:T(256)S(1)}, s32[]{:T(128)}, /*index=5*/bf16[192,128,128]{2,1,0:T(8,128...) while((s32[]{:T(128)}, f32[32,128,512]{2,1,0:T(8,128)}, ...), condition=%wide.region_3.4_spmd, body=%wide.region_1.3_spmd.sunk | while | flops 539493632 | bytes 47191152 | solution.py:49
  175.5 6.1 gather_fusion
  181.6 7.0 fusion.29
  188.7 18.8 %scatter_fusion = f32[32,128,512]{2,1,0:T(8,128)} fusion(f32[32,128,512]{2,1,0:T(8,128)} %get-tuple-element.257, s32[32]{0:T(128)S(1)} %get-tuple-element.232, f32[32,128,512]{2,1,0:T(8,128)} %fusion.29), kind=kCustom, calls=%fused_computation.3.clone.1 | custom fusion | flops 2097152 | bytes 25165952 | tf_op jit(solution)/shard_map/while/body/scatter-add | solution.py:42
  208.2 6.1 gather_fusion
  214.3 7.0 fusion.29
  221.4 18.5 %scatter_fusion = f32[32,128,512]{2,1,0:T(8,128)} fusion(f32[32,128,512]{2,1,0:T(8,128)} %get-tuple-element.257, s32[32]{0:T(128)S(1)} %get-tuple-element.232, f32[32,128,512]{2,1,0:T(8,128)} %fusion.29), kind=kCustom, calls=%fused_computation.3.clone.1 | custom fusion | flops 2097152 | bytes 25165952 | tf_op jit(solution)/shard_map/while/body/scatter-add | solution.py:42
  246.7 7.0 fusion.29
  253.7 18.1 %scatter_fusion = f32[32,128,512]{2,1,0:T(8,128)} fusion(f32[32,128,512]{2,1,0:T(8,128)} %get-tuple-element.257, s32[32]{0:T(128)S(1)} %get-tuple-element.232, f32[32,128,512]{2,1,0:T(8,128)} %fusion.29), kind=kCustom, calls=%fused_computation.3.clone.1 | custom fusion | flops 2097152 | bytes 25165952 | tf_op jit(solution)/shard_map/while/body/scatter-add | solution.py:42
  271.9 8.6 copy.10
  280.5 279.2 %all-reduce.3.cloned.1.call-done = f32[4096,512]{1,0:T(8,128)} async-done(((f32[4096,512]{1,0:T(8,128)}), f32[4096,512]{1,0:T(8,128)}) %all-reduce.3.cloned.1.call-update) | async-done | bytes 8388624 | tf_op jit(solution)/shard_map/psum | solution.py:75
  559.7 7.6 multiply_convert_fusion
  567.4 7.9 broadcast_in_dim.38
  575.2 94.5 %while.21 = (s32[]{:T(128)}, f32[64,128,512]{2,1,0:T(8,128)}, s32[]{:T(128)}, s32[192]{0:T(256)S(1)}, s32[]{:T(128)}, /*index=5*/bf16[192,128,128]{1,2,0:T(8,128...) while((s32[]{:T(128)}, f32[64,128,512]{2,1,0:T(8,128)}, ...), condition=%wide.region_7.8_spmd, body=%wide.region_5.7_spmd.sunk | while | flops 539493632 | bytes 47191152 | solution.py:49
  581.1 7.0 fusion.32
  588.1 18.6 %scatter_fusion.1 = f32[64,128,512]{2,1,0:T(8,128)} fusion(f32[64,128,512]{2,1,0:T(8,128)} %get-tuple-element.293, s32[32]{0:T(128)S(1)} %get-tuple-element.242, f32[32,128,512]{2,1,0:T(8,128)} %fusion.32), kind=kCustom, calls=%fused_computation.4.clone.1 | custom fusion | flops 2097152 | bytes 25165952 | tf_op jit(solution)/shard_map/while/body/scatter-add | solution.py:47
  612.5 7.0 fusion.32
  619.5 18.6 %scatter_fusion.1 = f32[64,128,512]{2,1,0:T(8,128)} fusion(f32[64,128,512]{2,1,0:T(8,128)} %get-tuple-element.293, s32[32]{0:T(128)S(1)} %get-tuple-element.242, f32[32,128,512]{2,1,0:T(8,128)} %fusion.32), kind=kCustom, calls=%fused_computation.4.clone.1 | custom fusion | flops 2097152 | bytes 25165952 | tf_op jit(solution)/shard_map/while/body/scatter-add | solution.py:47
  644.0 7.0 fusion.32
  651.0 18.7 %scatter_fusion.1 = f32[64,128,512]{2,1,0:T(8,128)} fusion(f32[64,128,512]{2,1,0:T(8,128)} %get-tuple-element.293, s32[32]{0:T(128)S(1)} %get-tuple-element.242, f32[32,128,512]{2,1,0:T(8,128)} %fusion.32), kind=kCustom, calls=%fused_computation.4.clone.1 | custom fusion | flops 2097152 | bytes 25165952 | tf_op jit(solution)/shard_map/while/body/scatter-add | solution.py:47
  669.8 189.1 %reduce-scatter.2.cloned.1.call-done = f32[512,512]{1,0:T(8,128)} async-done(((f32[8192,512]{1,0:T(8,128)}), f32[512,512]{1,0:T(8,128)}) %reduce-scatter.2.cloned.1.call-update) | async-done | bytes 1048592 | tf_op jit(solution)/shard_map/reduce_scatter | solution.py:82
  864.5 147.4 %all-reduce.5.cloned.1.call-done = f32[512,512]{1,0:T(8,128)} async-done(((f32[512,512]{1,0:T(8,128)}), f32[512,512]{1,0:T(8,128)}) %all-reduce.5.cloned.1.call-update) | async-done | bytes 1048592 | tf_op jit(solution)/shard_map/psum | solution.py:89
  (54 shorter events, 56.7 us)
Async XLA Ops:
  7.2 4.5 copy-start
  37.8 5.7 copy-start.2
  43.5 127.0 %all-to-all-start.1 = ((bf16[16,512,512]{2,1,0:T(8,128)(2,1)}), bf16[16,512,512]{2,1,0:T(8,128)(2,1)}, u32[]{:S(2)}, u32[]{:S(2)}) async-start(bf16[16,512,512]{2,1,0:T(8,128)(2,1)} %stack.2), calls=%async_computation.1 | async-start | bytes 16777216 | tf_op jit(solution)/shard_map/all_to_all | solution.py:69
  49.6 125.2 %copy-start.4 = (s32[1,1,192]{2,1,0:T(1,128)S(1)}, s32[1,1,192]{2,1,0:T(1,128)}, u32[]{:S(2)}) copy-start(s32[1,1,192]{2,1,0:T(1,128)} %param.16) | copy-start | bytes 2308
  49.6 125.2 %copy-start.5 = (s32[1,1,192]{2,1,0:T(1,128)S(1)}, s32[1,1,192]{2,1,0:T(1,128)}, u32[]{:S(2)}) copy-start(s32[1,1,192]{2,1,0:T(1,128)} %param.17) | copy-start | bytes 2308
  49.6 510.1 %all-reduce.3.cloned.1.call-start = ((), (), s32[]{:S(2)}) async-start(), calls=%async_computation.3 | async-start | bytes 16777216 | tf_op jit(solution)/shard_map/psum | solution.py:75
  271.8 587.1 %reduce-scatter.2.cloned.1.call-start = ((), (), s32[]{:S(2)}) async-start(), calls=%async_computation.4 | async-start | bytes 17825792 | tf_op jit(solution)/shard_map/reduce_scatter | solution.py:82
  669.7 344.5 %copy-start.1 = (bf16[512,512]{1,0:T(8,128)(2,1)S(1)}, bf16[512,512]{1,0:T(8,128)(2,1)}, u32[]{:S(2)}) copy-start(bf16[512,512]{1,0:T(8,128)(2,1)} %param.12) | copy-start | bytes 1572868
  669.7 189.2 %copy-start.3 = (bf16[512,512]{1,0:T(8,128)(2,1)S(1)}, bf16[512,512]{1,0:T(8,128)(2,1)}, u32[]{:S(2)}) copy-start(bf16[512,512]{1,0:T(8,128)(2,1)} %copy-done.2) | copy-start | bytes 1572868
  669.8 342.1 %all-reduce.5.cloned.1.call-start = ((), (), s32[]{:S(2)}) async-start(), calls=%async_computation.5 | async-start | bytes 2097152 | tf_op jit(solution)/shard_map/psum | solution.py:89
Sparse Core Ops, SparseCore 0:
  271.9 287.7 all-reduce.2
  669.9 188.9 reduce-scatter.1
  864.3 147.5 all-reduce.4
